TPU v7x, 1024 devices: a whole 4x4x32 slice. The times are simulated.
1024 devices in a mesh: dp: 128 (over x, z_hi, y, core), tensor: 8 (over z_lo).
Axes of the slice: x: 4, y: 4, z: 32 (z_hi: 4, z_lo: 8; z = z_hi * 8 + z_lo), core: 2. Of those that a mesh axis runs over, the one named last changes fastest.
Arguments:
- image_emb: bfloat16 [131072, 1152], P('dp', 'tensor'), may hold values from -0.19921875 to 0.19921875
- text_emb: bfloat16 [131072, 1152], P(('dp', 'tensor')), may hold values from -0.19921875 to 0.19921875
- partner: int32 [131072], P('dp'), may hold values from 0 to 131071, as said below
- log_scale: float32 [1], replicated, may hold values from 2 to 2.8
- logit_bias: float32 [1], replicated, may hold values from -7 to -5
Outputs:
- image_grad: bfloat16 [131072, 1152], P(('dp', 'tensor'))
- text_grad: bfloat16 [131072, 1152], P(('dp', 'tensor'))
- text_loss: float32 [131072], P(('dp', 'tensor'))
Inputs may be any that keep to these rules, and one draw needn't show every extreme that they name: `partner`: every image row in block b names a text row of the same block b, and within each block every text row is named by exactly one image row.
All inputs are finite; a program needn't handle non-finite values.
Results may differ from a plain program's by a relative error of at most 0.017.
Values may be sent and summed in bfloat16 or wider, within the bound.
A program may use at most 32 MiB of HBM per device.

v0:
```python
import jax
import jax.numpy as jnp
from jax import lax
from jax.sharding import PartitionSpec as P

epsilon = 1e-06


def from_behind(x, axis, by):
    size = lax.axis_size(axis)
    return lax.ppermute(x, axis, [(i, (i + by) % size) for i in range(size)])


def unit_rows(raw):
    values = raw.astype(jnp.float32)
    scales = lax.rsqrt(jnp.sum(values * values, axis=-1, keepdims=True) + epsilon)
    return (values * scales, scales)


def normal_back(delta, units, scales):
    return scales * (delta - units * jnp.sum(units * delta, axis=-1, keepdims=True))


def pass_text(block, offset):
    return from_behind(block, "dp", offset)


def return_grads(grads, losses, offset):
    return (
        from_behind(grads.astype(jnp.bfloat16), "dp", offset).astype(grads.dtype),
        from_behind(losses.astype(jnp.bfloat16), "dp", offset).astype(losses.dtype),
    )


def local(image_emb, text_emb, partner, log_scale, logit_bias):
    loop_size = lax.axis_size("dp")
    window = min(4, loop_size // 2)
    images = lax.all_gather(image_emb, "tensor", axis=1, tiled=True)
    row_count = images.shape[0]
    share_rows = text_emb.shape[0]
    image_units, image_scales = unit_rows(images)
    image_low = image_units.astype(jnp.bfloat16)
    temper = jnp.exp(log_scale[0])
    offset_bias = logit_bias[0]
    loop_index = lax.axis_index("dp")
    tensor_index = lax.axis_index("tensor")
    grad_tiles = []
    unit_list = []
    text_parts = []
    loss_parts = []
    current = text_emb
    for step in range(window):
        if step == 0:
            block = text_emb
        else:
            block = pass_text(current, 1)
        current = block
        owner = (loop_index - step) % loop_size
        first = owner * row_count + tensor_index * share_rows
        columns = first + jnp.arange(share_rows, dtype=jnp.int32)
        text_units, text_scales = unit_rows(block)
        text_low = text_units.astype(jnp.bfloat16)
        logits = (
            temper
            * lax.dot_general(
                image_low, text_low, (((1,), (1,)), ((), ())), preferred_element_type=jnp.float32
            )
            + offset_bias
        )
        labels = jnp.where(partner[:, None] == columns[None, :], 1.0, -1.0).astype(jnp.float32)
        loss_parts.append(jnp.sum(jax.nn.softplus(-labels * logits), axis=0))
        grad_tile = (-labels * jax.nn.sigmoid(-labels * logits)).astype(jnp.bfloat16)
        delta = temper * lax.dot_general(
            grad_tile, image_low, (((0,), (0,)), ((), ())), preferred_element_type=jnp.float32
        )
        text_parts.append(normal_back(delta, text_units, text_scales))
        grad_tiles.append(grad_tile)
        unit_list.append(text_low)
    carried_grad = text_parts[window - 1]
    carried_loss = loss_parts[window - 1]
    for step in range(window - 2, 0, -1):
        moved = return_grads(carried_grad, carried_loss, -1)
        carried_grad = moved[0] + text_parts[step]
        carried_loss = moved[1] + loss_parts[step]
    moved = return_grads(carried_grad, carried_loss, -1)
    grad_total = text_parts[0] + moved[0]
    loss_total = loss_parts[0] + moved[1]
    tiles_all = jnp.concatenate(grad_tiles, axis=1)
    units_all = jnp.concatenate(unit_list, axis=0)
    delta_rows = temper * jnp.dot(tiles_all, units_all, preferred_element_type=jnp.float32)
    units, scales = unit_rows(images)
    image_sum = lax.psum_scatter(
        normal_back(delta_rows, units, scales).astype(jnp.bfloat16),
        "tensor",
        scatter_dimension=0,
        tiled=True,
    )
    return (image_sum, grad_total.astype(jnp.bfloat16), loss_total)


def solution(mesh):
    placed = (P("dp", "tensor"), P(("dp", "tensor"), None), P("dp"), P(), P())
    return jax.shard_map(
        local,
        mesh=mesh,
        in_specs=placed,
        out_specs=(P(("dp", "tensor"), None), P(("dp", "tensor"), None), P(("dp", "tensor"))),
        check_vma=False,
    )
```

profile of v0, /device:TPU:61, one launch (start us, length us, event | category | flops | bytes accessed | tf_op | source)
XLA Modules:
  0.0 309.8 jit_solution(8775751257304925308)
XLA Ops:
  7.9 15.7 %collective-permute-start = (bf16[128,1152]{1,0:T(8,128)(2,1)}, bf16[128,1152]{1,0:T(8,128)(2,1)S(1)}, u32[]{:S(2)}, u32[]{:S(2)}) collective-permute-start(bf16[128,1152]{1,0:T(8,128)(2,1)} %param.6), channel_id=1, source_target_pairs={{0,8},{8,16},{16,24},{24,32},{32,40},{40,48},{48,56},{56,64},{64,7... | collective-permute-start | bytes 884744 | tf_op jit(solution)/shard_map/ppermute | solution.py:11
  29.3 5.5 %collective-permute-done = bf16[128,1152]{1,0:T(8,128)(2,1)S(1)} collective-permute-done((bf16[128,1152]{1,0:T(8,128)(2,1)}, bf16[128,1152]{1,0:T(8,128)(2,1)S(1)}, u32[]{:S(2)}, u32[]{:S(2)}) %collective-permute-start) | collective-permute-done | bytes 294944 | tf_op jit(solution)/shard_map/ppermute | solution.py:11
  34.8 15.6 %collective-permute-start.1 = (bf16[128,1152]{1,0:T(8,128)(2,1)S(1)}, bf16[128,1152]{1,0:T(8,128)(2,1)S(1)}, u32[]{:S(2)}, u32[]{:S(2)}) collective-permute-start(bf16[128,1152]{1,0:T(8,128)(2,1)S(1)} %collective-permute-done), channel_id=1, source_target_pairs={{0,8},{8,16},{16,24},{24,32},{32,40},{40,48},{48,56},{56,64},{64,7... | collective-permute-start | bytes 884744 | tf_op jit(solution)/shard_map/ppermute | solution.py:11
  51.4 31.5 %collective-permute-done.1 = bf16[128,1152]{1,0:T(8,128)(2,1)S(1)} collective-permute-done((bf16[128,1152]{1,0:T(8,128)(2,1)S(1)}, bf16[128,1152]{1,0:T(8,128)(2,1)S(1)}, u32[]{:S(2)}, u32[]{:S(2)}) %collective-permute-start.1) | collective-permute-done | bytes 294944 | tf_op jit(solution)/shard_map/ppermute | solution.py:11
  83.0 17.7 %collective-permute-start.2 = (bf16[128,1152]{1,0:T(8,128)(2,1)S(1)}, bf16[128,1152]{1,0:T(8,128)(2,1)S(1)}, u32[]{:S(2)}, u32[]{:S(2)}) collective-permute-start(bf16[128,1152]{1,0:T(8,128)(2,1)S(1)} %collective-permute-done.1), channel_id=1, source_target_pairs={{0,8},{8,16},{16,24},{24,32},{32,40},{40,48},{48,56},{56,64},{64,7... | collective-permute-start | bytes 884744 | tf_op jit(solution)/shard_map/ppermute | solution.py:11
  101.7 19.8 %collective-permute-done.2 = bf16[128,1152]{1,0:T(8,128)(2,1)S(1)} collective-permute-done((bf16[128,1152]{1,0:T(8,128)(2,1)S(1)}, bf16[128,1152]{1,0:T(8,128)(2,1)S(1)}, u32[]{:S(2)}, u32[]{:S(2)}) %collective-permute-start.2) | collective-permute-done | bytes 294944 | tf_op jit(solution)/shard_map/ppermute | solution.py:11
  122.5 23.1 %all-gather.2.cloned.1.call-done = bf16[1024,1152]{0,1:T(8,128)(2,1)} async-done(((bf16[1024,144]{0,1:T(8,128)(2,1)}), bf16[1024,1152]{0,1:T(8,128)(2,1)}) %all-gather.2.cloned.1.call-update) | async-done | bytes 2359312 | tf_op jit(solution)/shard_map/all_gather | solution.py:38
  145.6 3.0 copy.9
  149.3 1.9 fusion.65
  151.2 1.8 fusion.68
  153.0 1.9 fusion.67
  154.9 1.8 fusion.66
  156.7 1.7 fusion.3
  158.5 2.3 fusion.6
  161.4 2.5 collective-permute-start.6
  165.0 2.1 collective-permute-start.3
  167.9 9.4 %collective-permute-done.6 = bf16[128]{0:T(256)(128)(2,1)S(1)} collective-permute-done((bf16[128]{0:T(256)(128)(2,1)S(1)}, bf16[128]{0:T(256)(128)(2,1)S(1)}, u32[]{:S(2)}, u32[]{:S(2)}) %collective-permute-start.6) | collective-permute-done | bytes 288 | tf_op jit(solution)/shard_map/ppermute | solution.py:11
  177.3 1.9 collective-permute-start.7
  179.2 24.0 %collective-permute-done.3 = bf16[128,1152]{1,0:T(8,128)(2,1)S(1)} collective-permute-done((bf16[128,1152]{1,0:T(8,128)(2,1)S(1)}, bf16[128,1152]{1,0:T(8,128)(2,1)S(1)}, u32[]{:S(2)}, u32[]{:S(2)}) %collective-permute-start.3) | collective-permute-done | bytes 294944 | tf_op jit(solution)/shard_map/ppermute | solution.py:11
  203.4 2.1 collective-permute-start.4
  206.3 1.9 collective-permute-start.8
  208.3 53.8 %collective-permute-done.4 = bf16[128,1152]{1,0:T(8,128)(2,1)S(1)} collective-permute-done((bf16[128,1152]{1,0:T(8,128)(2,1)S(1)}, bf16[128,1152]{1,0:T(8,128)(2,1)S(1)}, u32[]{:S(2)}, u32[]{:S(2)}) %collective-permute-start.4) | collective-permute-done | bytes 294944 | tf_op jit(solution)/shard_map/ppermute | solution.py:11
  262.3 1.9 collective-permute-start.5
  265.6 36.5 %collective-permute-done.5 = bf16[128,1152]{1,0:T(8,128)(2,1)S(1)} collective-permute-done((bf16[128,1152]{1,0:T(8,128)(2,1)S(1)}, bf16[128,1152]{1,0:T(8,128)(2,1)S(1)}, u32[]{:S(2)}, u32[]{:S(2)}) %collective-permute-start.5) | collective-permute-done | bytes 294944 | tf_op jit(solution)/shard_map/ppermute | solution.py:11
  (82 shorter events, 14.8 us)
Async XLA Ops:
  7.2 138.4 %all-gather.2.cloned.1.call-start = ((), (), s32[]{:S(2)}) async-start(), calls=%async_computation.1 | async-start | bytes 2654208 | tf_op jit(solution)/shard_map/all_gather | solution.py:38
  7.9 295.1 %reduce-scatter.2.cloned.1.call-start = ((), (), s32[]{:S(2)}) async-start(), calls=%async_computation.2 | async-start | bytes 2654208 | tf_op jit(solution)/shard_map/reduce_scatter | solution.py:92
  7.9 26.9 %collective-permute-start = (bf16[128,1152]{1,0:T(8,128)(2,1)}, bf16[128,1152]{1,0:T(8,128)(2,1)S(1)}, u32[]{:S(2)}, u32[]{:S(2)}) collective-permute-start(bf16[128,1152]{1,0:T(8,128)(2,1)} %param.6), channel_id=1, source_target_pairs={{0,8},{8,16},{16,24},{24,32},{32,40},{40,48},{48,56},{56,64},{64,7... | collective-permute-start | bytes 884744 | tf_op jit(solution)/shard_map/ppermute | solution.py:11
  34.8 48.1 %collective-permute-start.1 = (bf16[128,1152]{1,0:T(8,128)(2,1)S(1)}, bf16[128,1152]{1,0:T(8,128)(2,1)S(1)}, u32[]{:S(2)}, u32[]{:S(2)}) collective-permute-start(bf16[128,1152]{1,0:T(8,128)(2,1)S(1)} %collective-permute-done), channel_id=1, source_target_pairs={{0,8},{8,16},{16,24},{24,32},{32,40},{40,48},{48,56},{56,64},{64,7... | collective-permute-start | bytes 884744 | tf_op jit(solution)/shard_map/ppermute | solution.py:11
  83.0 38.5 %collective-permute-start.2 = (bf16[128,1152]{1,0:T(8,128)(2,1)S(1)}, bf16[128,1152]{1,0:T(8,128)(2,1)S(1)}, u32[]{:S(2)}, u32[]{:S(2)}) collective-permute-start(bf16[128,1152]{1,0:T(8,128)(2,1)S(1)} %collective-permute-done.1), channel_id=1, source_target_pairs={{0,8},{8,16},{16,24},{24,32},{32,40},{40,48},{48,56},{56,64},{64,7... | collective-permute-start | bytes 884744 | tf_op jit(solution)/shard_map/ppermute | solution.py:11
  121.6 26.9 %copy-start.4 = (f32[128]{0:T(128)}, f32[128]{0:T(128)S(1)}, u32[]{:S(2)}) copy-start(f32[128]{0:T(128)S(1)} %add_rsqrt_fusion.1) | copy-start | bytes 1540
  151.1 5.5 %copy-start.15 = (bf16[1024,128]{1,0:T(8,128)(2,1)}, bf16[1024,128]{1,0:T(8,128)(2,1)S(1)}, u32[]{:S(2)}) copy-start(bf16[1024,128]{1,0:T(8,128)(2,1)S(1)} %get-tuple-element.10) | copy-start | bytes 786436
  153.0 3.7 %copy-start.17 = (bf16[1024,128]{1,0:T(8,128)(2,1)}, bf16[1024,128]{1,0:T(8,128)(2,1)S(1)}, u32[]{:S(2)}) copy-start(bf16[1024,128]{1,0:T(8,128)(2,1)S(1)} %get-tuple-element.8) | copy-start | bytes 786436
  153.0 1.9 copy-start.3
  160.8 3.2 %copy-start.5 = (f32[128]{0:T(128)S(1)}, f32[128]{0:T(128)}, u32[]{:S(2)}) copy-start(f32[128]{0:T(128)} %copy-done.4) | copy-start | bytes 1540
  160.8 3.2 %copy-start.22 = (bf16[1024,128]{1,0:T(8,128)(2,1)S(1)}, bf16[1024,128]{1,0:T(8,128)(2,1)}, u32[]{:S(2)}) copy-start(bf16[1024,128]{1,0:T(8,128)(2,1)} %copy-done.21) | copy-start | bytes 786436
  161.4 5.6 %copy-start.20 = (bf16[1024,128]{1,0:T(8,128)(2,1)S(1)}, bf16[1024,128]{1,0:T(8,128)(2,1)}, u32[]{:S(2)}) copy-start(bf16[1024,128]{1,0:T(8,128)(2,1)} %copy-done.19) | copy-start | bytes 786436
  161.4 15.8 %collective-permute-start.6 = (bf16[128]{0:T(256)(128)(2,1)S(1)}, bf16[128]{0:T(256)(128)(2,1)S(1)}, u32[]{:S(2)}, u32[]{:S(2)}) collective-permute-start(bf16[128]{0:T(256)(128)(2,1)S(1)} %copy-done.7), channel_id=1, source_target_pairs={{0,1016},{8,0},{16,8},{24,16},{32,24},{40,32},{48,40},{56,48},{64,... | collective-permute-start | bytes 776 | tf_op jit(solution)/shard_map/ppermute | solution.py:11
  164.7 12.5 %copy-start.10 = (f32[128]{0:T(128)S(1)}, f32[128]{0:T(128)}, u32[]{:S(2)}) copy-start(f32[128]{0:T(128)} %get-tuple-element.5) | copy-start | bytes 1540
  165.0 40.5 %copy-start.18 = (bf16[1024,128]{1,0:T(8,128)(2,1)S(1)}, bf16[1024,128]{1,0:T(8,128)(2,1)}, u32[]{:S(2)}) copy-start(bf16[1024,128]{1,0:T(8,128)(2,1)} %copy-done.17) | copy-start | bytes 786436
  165.0 38.2 %collective-permute-start.3 = (bf16[128,1152]{1,0:T(8,128)(2,1)S(1)}, bf16[128,1152]{1,0:T(8,128)(2,1)S(1)}, u32[]{:S(2)}, u32[]{:S(2)}) collective-permute-start(bf16[128,1152]{1,0:T(8,128)(2,1)S(1)} %fusion.63), channel_id=1, source_target_pairs={{0,1016},{8,0},{16,8},{24,16},{32,24},{40,32},{48,40},{56,48},{64,... | collective-permute-start | bytes 884744 | tf_op jit(solution)/shard_map/ppermute | solution.py:11
  177.3 29.0 %collective-permute-start.7 = (bf16[128]{0:T(256)(128)(2,1)S(1)}, bf16[128]{0:T(256)(128)(2,1)S(1)}, u32[]{:S(2)}, u32[]{:S(2)}) collective-permute-start(bf16[128]{0:T(256)(128)(2,1)S(1)} %add_convert_fusion.1), channel_id=1, source_target_pairs={{0,1016},{8,0},{16,8},{24,16},{32,24},{40,32},{48,40},{56,48},{64,... | collective-permute-start | bytes 776 | tf_op jit(solution)/shard_map/ppermute | solution.py:11
  203.2 3.1 %copy-start.9 = (f32[128]{0:T(128)S(1)}, f32[128]{0:T(128)}, u32[]{:S(2)}) copy-start(f32[128]{0:T(128)} %get-tuple-element.7) | copy-start | bytes 1540
  203.4 60.8 %copy-start = (bf16[128,1152]{1,0:T(8,128)(2,1)S(1)}, bf16[128,1152]{1,0:T(8,128)(2,1)}, u32[]{:S(2)}) copy-start(bf16[128,1152]{1,0:T(8,128)(2,1)} %param.6) | copy-start | bytes 884740
  203.4 60.8 %copy-start.16 = (bf16[1024,128]{1,0:T(8,128)(2,1)S(1)}, bf16[1024,128]{1,0:T(8,128)(2,1)}, u32[]{:S(2)}) copy-start(bf16[1024,128]{1,0:T(8,128)(2,1)} %copy-done.15) | copy-start | bytes 786436
  203.4 58.6 %collective-permute-start.4 = (bf16[128,1152]{1,0:T(8,128)(2,1)S(1)}, bf16[128,1152]{1,0:T(8,128)(2,1)S(1)}, u32[]{:S(2)}, u32[]{:S(2)}) collective-permute-start(bf16[128,1152]{1,0:T(8,128)(2,1)S(1)} %fusion.58), channel_id=1, source_target_pairs={{0,1016},{8,0},{16,8},{24,16},{32,24},{40,32},{48,40},{56,48},{64,... | collective-permute-start | bytes 884744 | tf_op jit(solution)/shard_map/ppermute | solution.py:11
  206.3 58.7 %collective-permute-start.8 = (bf16[128]{0:T(256)(128)(2,1)S(1)}, bf16[128]{0:T(256)(128)(2,1)S(1)}, u32[]{:S(2)}, u32[]{:S(2)}) collective-permute-start(bf16[128]{0:T(256)(128)(2,1)S(1)} %add_convert_fusion), channel_id=1, source_target_pairs={{0,1016},{8,0},{16,8},{24,16},{32,24},{40,32},{48,40},{56,48},{64,... | collective-permute-start | bytes 776 | tf_op jit(solution)/shard_map/ppermute | solution.py:11
  262.0 3.0 copy-start.8
  262.3 39.7 %collective-permute-start.5 = (bf16[128,1152]{1,0:T(8,128)(2,1)S(1)}, bf16[128,1152]{1,0:T(8,128)(2,1)S(1)}, u32[]{:S(2)}, u32[]{:S(2)}) collective-permute-start(bf16[128,1152]{1,0:T(8,128)(2,1)S(1)} %fusion.52), channel_id=1, source_target_pairs={{0,1016},{8,0},{16,8},{24,16},{32,24},{40,32},{48,40},{56,48},{64,... | collective-permute-start | bytes 884744 | tf_op jit(solution)/shard_map/ppermute | solution.py:11
  (10 other events, 14.9 us)
Sparse Core Ops, SparseCore 0:
  10.7 134.8 all-gather.1
  160.9 78.2 reduce-scatter.1
where the time goes:
time: 310 us
  waiting for transfers between devices  204 us (66%)
  starting transfers between devices  61.4 us (20%)
  between operations  15.7 us (5%)
  other arithmetic  12.3 us (4%)
  matrix products  12.3 us (4%)
  local copies, waits for them, and re-layouts  3.84 us (1%)
    ppermute x9, waiting for transfers between devices, from_behind(): return lax.ppermute(x, axis, [(i, (i + by) % size) for i in range(size)])  180 us
    ppermute x9, starting transfers between devices, from_behind(): return lax.ppermute(x, axis, [(i, (i + by) % size) for i in range(size)])  61.3 us
    all_gather x1, waiting for transfers between devices, local(): images = lax.all_gather(image_emb, 'tensor', axis=1, tiled=True)  23.1 us
    dot_general x4, matrix products, local(): lax.dot_general(image_low, text_low, (((1,), (1,)), ((), ())), preferred_...  7.34 us
  transfers between devices with their start and end apart: 11, of which 8 were waited for; matrix products, arithmetic and copies ran while one was open for 4% of the time, Pallas kernels for 0%

commit v1 on v0

v1 whole, which is shorter than its diff:
```python
import functools

import jax
import jax.numpy as jnp
from jax import lax
from jax.experimental import pallas as pl
from jax.experimental.pallas import tpu as pltpu
from jax.sharding import PartitionSpec as P

MESH = pl.DeviceIdType.MESH
epsilon = 1e-06
N_T = 8
N_DP = 128
GROUP = 8
ROWS = 1024
SHARE = ROWS // N_T
WIDTH = 1152
SLICE = WIDTH // N_T
STEPS = 4
CHUNKS = 4
LANES = ROWS // CHUNKS
PARTS = 4
WINDOW_STEPS = 46
PART = WIDTH // PARTS
STRIP = SHARE // GROUP
PAIRS = ((0, 0), (0, 1), (0, 2), (1, 0), (1, 1), (2, 0))
CARRY = WIDTH + 128
ORDER = (7, 0, 6, 1, 5, 2, 4, 3)


def kernel(
    img_ref, txt_ref, partner_ref, scale_ref, bias_ref,
    image_out, text_out, loss_out,
    images, texts, low, low_t, delta, cross, loss, piece, from_left, from_right,
    chain_out, chain_back, contrib, returned, shares,
    ag_send, ag_recv, rs_send, rs_recv, tx_send, tx_recv, spread_send, spread_recv,
    out_send, out_recv, fan_send, gr_send, gr_recv, share_send, share_recv,
    back_send, back_recv, home_send,
):
    d = lax.axis_index("dp")
    t = lax.axis_index("tensor")
    q = lax.rem(d, GROUP)
    base = d - q
    up = (jnp.where(t == N_T - 1, lax.rem(d + GROUP, N_DP), d), lax.rem(t + 1, N_T))
    down = (jnp.where(t == 0, lax.rem(d + N_DP - GROUP, N_DP), d), lax.rem(t + N_T - 1, N_T))

    def copy(src, dst, send_sem, recv_sem, where):
        return pltpu.make_async_remote_copy(
            src_ref=src, dst_ref=dst, send_sem=send_sem, recv_sem=recv_sem,
            device_id=where, device_id_type=MESH,
        )

    def arrived(view, sem):
        copy(view, view, home_send.at[0], sem, up).wait_recv()

    def left(view, sem):
        copy(view, view, sem, gr_recv.at[0], up).wait_send()

    def mate(other):
        return lax.rem(q + other, GROUP)

    def strip(p):
        return pl.ds(pl.multiple_of(p * STRIP, STRIP), STRIP)

    barrier = pltpu.get_barrier_semaphore()
    for other in range(1, GROUP):
        pl.semaphore_signal(barrier, inc=1, device_id=(base + mate(other), t), device_id_type=MESH)
    pl.semaphore_signal(barrier, inc=1, device_id=up, device_id_type=MESH)
    pl.semaphore_signal(barrier, inc=1, device_id=down, device_id_type=MESH)
    pl.semaphore_wait(barrier, GROUP - 1 + 2)

    images[t] = img_ref[...]

    def image_view(way, s, r):
        return images.at[t - s if way == 0 else t + s, :, pl.ds(r * LANES, LANES)]

    def image_copy(way, s, r):
        view = image_view(way, s, r)
        to = t + 1 if way == 0 else t - 1
        return copy(view, view, ag_send.at[way, s, r], ag_recv.at[way, s + 1, r], (d, to))

    def gather_step(pair, s, first=False):
        for r in (2 * pair, 2 * pair + 1):
            @pl.when(t >= s)
            def _():
                if not first:
                    arrived(image_view(0, s, r), ag_recv.at[0, s, r])

                @pl.when(t < N_T - 1)
                def _():
                    image_copy(0, s, r).start()

            @pl.when(t + s < N_T)
            def _():
                if not first:
                    arrived(image_view(1, s, r), ag_recv.at[1, s, r])

                @pl.when(t > 0)
                def _():
                    image_copy(1, s, r).start()

    def text_copy(k):
        return copy(txt_ref, texts.at[k], tx_send.at[k], tx_recv.at[k], (lax.rem(d + k, N_DP), t))

    def spread(b, other):
        return copy(
            txt_ref.at[strip(mate(other))], chain_out.at[0, b],
            spread_send, spread_recv, (base + mate(other), t),
        )

    for b in range(STEPS - 1):
        @pl.when(q == GROUP - 1 - b)
        def _():
            for other in range(1, GROUP):
                spread(b, other).start()
            chain_out[0, b] = txt_ref[strip(q), :]

    gather_step(0, 0, True)
    for k in range(1, STEPS):
        @pl.when(q + k < GROUP)
        def _():
            text_copy(k).start()

    def hop_out(h):
        return copy(chain_out.at[h], chain_out.at[h + 1], out_send.at[h], out_recv.at[h + 1], up)

    @pl.when(q < GROUP - 3)
    def _():
        arrived(chain_out.at[0], spread_recv)

    @pl.when(q >= GROUP - 3)
    def _():
        arrived(chain_out.at[0, pl.ds(0, 2)], spread_recv)

    hop_out(0).start()

    def first_pair(s, carry):
        gather_step(0, s)
        arrived(chain_out.at[s], out_recv.at[s])
        hop_out(s).start()
        return carry

    lax.fori_loop(1, N_T, first_pair, 0)
    gather_step(1, 0, True)
    arrived(chain_out.at[N_T], out_recv.at[N_T])

    def fan(b, e):
        k = 1 + b + e
        return copy(
            chain_out.at[N_T, b], texts.at[k, strip(q)],
            fan_send.at[b, e], tx_recv.at[k], (base + e, t),
        )

    for b, e in PAIRS:
        @pl.when(q != e)
        def _():
            fan(b, e).start()

        @pl.when(q == e)
        def _():
            texts[1 + b + e, strip(q), :] = chain_out[N_T, b]

    temper_row = jnp.exp(jnp.full((1, 128), scale_ref[0], jnp.float32))
    temper = temper_row[:, :1]
    bias = bias_ref[0]

    def text_units(k):
        raw = (txt_ref[...] if k == 0 else texts[k]).astype(jnp.float32)
        scales = lax.rsqrt(jnp.sum(raw * raw, axis=1, keepdims=True) + epsilon)
        return raw * scales, scales

    for k in range(STEPS):
        if k > 0:
            @pl.when(q >= k)
            def _():
                arrived(texts.at[k], tx_recv.at[k])

            @pl.when(q < k)
            def _():
                arrived(texts.at[k, pl.ds(0, SHARE - STRIP)], tx_recv.at[k])

        units, _ = text_units(k)
        low[pl.ds(k * SHARE, SHARE), :] = units.astype(jnp.bfloat16)
        low_t[:, pl.ds(k * SHARE, SHARE)] = units.T.astype(jnp.bfloat16)
    delta[...] = jnp.zeros_like(delta)
    cross[...] = jnp.zeros_like(cross)
    loss[...] = jnp.zeros_like(loss)

    def compute(r, carry):
        lanes = pl.ds(pl.multiple_of(r * LANES, LANES), LANES)
        raw = images[:, :, lanes].reshape(WIDTH, LANES).astype(jnp.float32)
        scales = lax.rsqrt(jnp.sum(raw * raw, axis=0, keepdims=True) + epsilon)
        unit = (raw * scales).astype(jnp.bfloat16)
        dots = jnp.dot(low[...], unit, preferred_element_type=jnp.float32)
        index = lax.broadcasted_iota(jnp.int32, (STEPS * SHARE, LANES), 0)
        step = index // SHARE
        block = d - step
        block = jnp.where(block < 0, block + N_DP, block)
        names = block * ROWS + t * SHARE + (index - step * SHARE)
        same = partner_ref[:, lanes] == names
        logits = temper * dots + bias
        z = jnp.where(same, -logits, logits)
        e = jnp.exp(z)
        u = 1.0 + e
        inverse = 1.0 / u
        sigmoid = e * inverse
        terms = jnp.log(u) + (e - (u - 1.0)) * inverse
        grad = jnp.where(same, -sigmoid, sigmoid).astype(jnp.bfloat16)
        along = grad.astype(jnp.float32) * dots
        loss[...] += terms[:, :128] + terms[:, 128:]
        cross[...] += along[:, :128] + along[:, 128:]
        delta[...] += lax.dot_general(
            grad, unit, (((1,), (1,)), ((), ())), preferred_element_type=jnp.float32
        )
        part = jnp.dot(low_t[...], grad, preferred_element_type=jnp.float32)
        back = jnp.sum(along, axis=0, keepdims=True)
        out = ((temper * scales) * (part - unit.astype(jnp.float32) * back)).astype(jnp.bfloat16)
        piece[7 - r] = out[:, :128]
        piece[r] = out[:, 128:]
        return carry

    def sum_rows(m):
        return pl.ds(pl.multiple_of(m * PART, 16), PART)

    def sum_copy(way, owner, m):
        held = from_left if way == 0 else from_right
        to = t + 1 if way == 0 else t - 1
        return copy(
            piece.at[owner, sum_rows(m)], held.at[owner, sum_rows(m)],
            rs_send.at[way, owner, m], rs_recv.at[way, owner, m], (d, to),
        )

    def sum_take(way, owner, m):
        held = from_left if way == 0 else from_right
        arrived(held.at[owner, sum_rows(m)], rs_recv.at[way, owner, m])
        total = piece[owner, sum_rows(m), :].astype(jnp.float32) + held[owner, sum_rows(m), :].astype(jnp.float32)
        piece[owner, sum_rows(m), :] = total.astype(jnp.bfloat16)

    def reduce_step(p, carry):
        for way in range(2):
            n = p - 2 * (t if way == 0 else N_T - 1 - t)

            @pl.when(jnp.logical_and(n >= 0, n < N_T * PARTS))
            def _():
                a = n // PARTS
                m = n - a * PARTS
                far = jnp.where(a % 2 == 0, N_T - 1 - a // 2, a // 2)
                owner = far if way == 0 else N_T - 1 - far

                @pl.when(owner >= t if way == 0 else owner <= t)
                def _():
                    @pl.when(t > 0 if way == 0 else t < N_T - 1)
                    def _():
                        sum_take(way, owner, m)

                    @pl.when(owner != t)
                    def _():
                        sum_copy(way, owner, m).start()

        return carry

    def second_pair(c, carry):
        gather_step(1, 2 * c + 1)
        compute(c, 0)
        gather_step(1, 2 * c + 2)
        return lax.fori_loop(4 * c, 4 * c + 4, reduce_step, carry)

    lax.fori_loop(0, 2, second_pair, 0)

    def last_slices(s, carry):
        gather_step(1, s)
        return lax.fori_loop(2 * s - 2, 2 * s, reduce_step, carry)

    lax.fori_loop(5, N_T, last_slices, 0)
    lax.fori_loop(2, 4, compute, 0)

    def text_result(k):
        rows = pl.ds(k * SHARE, SHARE)
        units, scales = text_units(k)
        back = jnp.sum(cross[rows, :], axis=1, keepdims=True)
        grads = (temper * scales) * (delta[rows, :] - units * back)
        return grads, jnp.sum(loss[rows, :], axis=1, keepdims=True)

    def grad_copy(k):
        return copy(
            contrib.at[k], returned.at[k], gr_send.at[k], gr_recv.at[k], (lax.rem(d + N_DP - k, N_DP), t)
        )

    def share_copy(k, slot, other):
        return copy(
            contrib.at[k, strip(mate(other))], shares.at[slot],
            share_send.at[k], share_recv, (base + mate(other), t),
        )

    for k in range(STEPS - 1, 0, -1):
        grads, total = text_result(k)
        contrib[k, :, pl.ds(0, WIDTH)] = grads.astype(jnp.bfloat16)
        contrib[k, :, pl.ds(WIDTH, 128)] = jnp.broadcast_to(total, (SHARE, 128)).astype(jnp.bfloat16)

        for slot, (b, e) in enumerate(PAIRS):
            if 1 + b + e == k:
                @pl.when(q == e)
                def _():
                    for other in range(1, GROUP):
                        share_copy(k, slot, other).start()
                    shares[slot] = contrib[k, strip(q), :]

        @pl.when(q >= k)
        def _():
            grad_copy(k).start()

    lax.fori_loop(14, 20, reduce_step, 0)

    def hop_back(h):
        return copy(chain_back.at[h], chain_back.at[h + 1], back_send.at[h], back_recv.at[h + 1], down)

    for e in range(STEPS - 1):
        @pl.when(q == e)
        def _():
            arrived(shares.at[pl.ds(0, STEPS - 1 + e)], share_recv)

    @pl.when(q >= STEPS - 1)
    def _():
        arrived(shares, share_recv)

    for b in range(STEPS - 1):
        total = None
        for slot, (bb, e) in enumerate(PAIRS):
            if bb == b:
                term = shares[slot].astype(jnp.float32)
                total = term if total is None else total + term
        chain_back[0, b] = total.astype(jnp.bfloat16)
    hop_back(0).start()

    def tail(h, carry):
        lax.fori_loop(17 + 3 * h, 20 + 3 * h, reduce_step, carry)
        arrived(chain_back.at[h], back_recv.at[h])
        hop_back(h).start()
        return carry

    lax.fori_loop(1, N_T, tail, 0)
    lax.fori_loop(41, WINDOW_STEPS, reduce_step, 0)
    arrived(chain_back.at[N_T], back_recv.at[N_T])

    def home(b):
        return copy(
            chain_back.at[N_T, b], returned.at[3, strip(q)],
            home_send.at[b], gr_recv.at[3], (base + GROUP - 1 - b, t),
        )

    for b in range(STEPS - 1):
        @pl.when(q != GROUP - 1 - b)
        def _():
            home(b).start()

        @pl.when(q == GROUP - 1 - b)
        def _():
            returned[3, strip(q), :] = chain_back[N_T, b]

    image_out[...] = piece[t].astype(jnp.float32).T.astype(jnp.bfloat16)

    grads, total = text_result(0)
    total = jnp.broadcast_to(total, (SHARE, 128))
    delta[pl.ds(0, SHARE), :] = grads
    loss[pl.ds(0, SHARE), :] = total

    def take(k):
        delta[pl.ds(0, SHARE), :] += returned[k, :, pl.ds(0, WIDTH)].astype(jnp.float32)
        loss[pl.ds(0, SHARE), :] += returned[k, :, pl.ds(WIDTH, 128)].astype(jnp.float32)

    for k in range(1, STEPS - 1):
        @pl.when(q + k < GROUP)
        def _():
            arrived(returned.at[k], gr_recv.at[k])
            take(k)

    @pl.when(q + 3 < GROUP)
    def _():
        arrived(returned.at[3], gr_recv.at[3])

    @pl.when(q + 3 >= GROUP)
    def _():
        arrived(returned.at[3, pl.ds(0, SHARE - STRIP)], gr_recv.at[3])

    take(3)
    text_out[...] = delta[pl.ds(0, SHARE), :].astype(jnp.bfloat16)
    loss_out[...] = loss[pl.ds(0, SHARE), :].T[:8]

    @pl.when(q >= GROUP - 3)
    def _():
        left(txt_ref.at[pl.ds(0, SHARE - STRIP)], spread_send)

    for b, e in PAIRS:
        @pl.when(q != e)
        def _():
            fan(b, e).wait_send()

    for b in range(STEPS - 1):
        @pl.when(q != GROUP - 1 - b)
        def _():
            home(b).wait_send()

    for k in range(1, STEPS):
        @pl.when(q + k < GROUP)
        def _():
            text_copy(k).wait_send()

        @pl.when(q < k)
        def _():
            left(contrib.at[k, pl.ds(0, SHARE - STRIP)], share_send.at[k])

        @pl.when(q >= k)
        def _():
            grad_copy(k).wait_send()

    def drain(s, carry):
        hop_out(s).wait_send()
        hop_back(s).wait_send()
        for r in range(CHUNKS):
            @pl.when(jnp.logical_and(t >= s, t < N_T - 1))
            def _():
                image_copy(0, s, r).wait_send()

            @pl.when(jnp.logical_and(t + s < N_T, t > 0))
            def _():
                image_copy(1, s, r).wait_send()

        for m in range(PARTS):
            @pl.when(s > t)
            def _():
                sum_copy(0, s, m).wait_send()

            @pl.when(s < t)
            def _():
                sum_copy(1, s, m).wait_send()

        return carry

    lax.fori_loop(0, N_T, drain, 0)


def local(image_emb, text_emb, partner, log_scale, logit_bias):
    by_owner = image_emb.reshape(N_T, SHARE, SLICE)
    ordered = jnp.concatenate([by_owner[o] for o in ORDER], axis=0).T
    pairs = partner.reshape(N_T, SHARE)
    pairs = jnp.concatenate([pairs[o] for o in ORDER]).reshape(1, ROWS)
    bf16, f32 = jnp.bfloat16, jnp.float32
    dma = pltpu.SemaphoreType.DMA
    vmem = pl.BlockSpec(memory_space=pltpu.VMEM)
    smem = pl.BlockSpec(memory_space=pltpu.SMEM)
    image_grad, text_grad, text_loss = pl.pallas_call(
        kernel,
        name="window_loss",
        out_shape=(
            jax.ShapeDtypeStruct((SHARE, WIDTH), bf16),
            jax.ShapeDtypeStruct((SHARE, WIDTH), bf16),
            jax.ShapeDtypeStruct((8, SHARE), f32),
        ),
        in_specs=[vmem, vmem, vmem, smem, smem],
        out_specs=(vmem, vmem, vmem),
        scratch_shapes=[
            pltpu.VMEM((N_T, SLICE, ROWS), bf16),
            pltpu.VMEM((STEPS, SHARE, WIDTH), bf16),
            pltpu.VMEM((STEPS * SHARE, WIDTH), bf16),
            pltpu.VMEM((WIDTH, STEPS * SHARE), bf16),
            pltpu.VMEM((STEPS * SHARE, WIDTH), f32),
            pltpu.VMEM((STEPS * SHARE, 128), f32),
            pltpu.VMEM((STEPS * SHARE, 128), f32),
            pltpu.VMEM((N_T, WIDTH, SHARE), bf16),
            pltpu.VMEM((N_T, WIDTH, SHARE), bf16),
            pltpu.VMEM((N_T, WIDTH, SHARE), bf16),
            pltpu.VMEM((N_T + 1, STEPS - 1, STRIP, WIDTH), bf16),
            pltpu.VMEM((N_T + 1, STEPS - 1, STRIP, CARRY), bf16),
            pltpu.VMEM((STEPS, SHARE, CARRY), bf16),
            pltpu.VMEM((STEPS, SHARE, CARRY), bf16),
            pltpu.VMEM((len(PAIRS), STRIP, CARRY), bf16),
            dma((2, N_T + 1, CHUNKS)), dma((2, N_T + 1, CHUNKS)),
            dma((2, N_T, PARTS)), dma((2, N_T, PARTS)),
            dma((STEPS,)), dma((STEPS,)), dma, dma,
            dma((N_T,)), dma((N_T + 1,)), dma((STEPS - 1, STEPS - 1)),
            dma((STEPS,)), dma((STEPS,)), dma((STEPS,)), dma,
            dma((N_T,)), dma((N_T + 1,)), dma((STEPS - 1,)),
        ],
        compiler_params=pltpu.CompilerParams(
            collective_id=0, has_side_effects=True, vmem_limit_bytes=56 * 2**20
        ),
    )(ordered, text_emb, pairs, log_scale, logit_bias)
    return image_grad, text_grad, text_loss[0]


def solution(mesh):
    placed = (P("dp", "tensor"), P(("dp", "tensor"), None), P("dp"), P(), P())
    return jax.shard_map(
        local,
        mesh=mesh,
        in_specs=placed,
        out_specs=(P(("dp", "tensor"), None), P(("dp", "tensor"), None), P(("dp", "tensor"))),
        check_vma=False,
    )
```

time: 310 us -> 186 us (0.60)
  the two profiles are of different devices: /device:TPU:61 before, /device:TPU:88 now
where the time goes in v1:
time: 186 us; the launch traced here: 185 us
  Pallas kernels  176 us (95%)
  local copies, waits for them, and re-layouts  7.64 us (4%)
  between operations  2.11 us (1%)
    pallas_call x1, Pallas kernels, local(): pl.pallas_call(kernel, name='window_loss', out_shape=(jax.ShapeDtypeStruc...  176 us
    unnamed x26, local copies, waits for them, and re-layouts  6.43 us

profile of v1, /device:TPU:88, one launch (start us, length us, event | category | flops | bytes accessed | tf_op | source)
XLA Modules:
  0.0 185.4 jit_solution(11894989507693189503)
XLA Ops:
  0.6 0.0 copy-start.4
  0.6 0.0 copy-start.2
  2.0 0.0 copy-done.4
  2.1 0.0 copy-start.3
  2.1 0.8 slice_dynamic-update-slice_fusion.7
  2.9 0.0 copy-done.3
  2.9 0.8 slice_dynamic-update-slice_fusion.6
  3.7 0.8 slice_dynamic-update-slice_fusion.5
  4.5 0.8 slice_dynamic-update-slice_fusion.4
  5.3 0.0 copy-done.2
  5.4 0.0 copy-start
  5.4 0.7 copy-done
  6.1 175.7 %window_loss.1 = (bf16[128,1152]{1,0:T(8,128)(2,1)}, bf16[128,1152]{1,0:T(8,128)(2,1)}, f32[8,128]{1,0:T(8,128)}) custom-call(bf16[144,1024]{1,0:T(8,128)(2,1)} %bitcast.4, bf16[128,1152]{1,0:T(8,128)(2,1)} %txt_ref.1, s32[1,1024]{1,0:T(1,128)} %bitcast.5, f32[1]{0:T(128)S(6)} %copy.25.scale_ref, f32[1]{0:T(128)S(6)} %copy.26.bias_ref), custom_call_target="tpu_custom_call" | custom-call | tf_op jit(solution)/shard_map/window_loss/pallas_call | solution.py:451
  181.8 1.2 slice_bitcast_fusion
  183.0 0.0 copy-start.1
  183.0 1.7 copy.27
  184.7 0.0 copy-done.1
  184.7 0.7 copy.28
  (13 shorter events, 0.1 us)
Async XLA Ops:
  0.6 1.4 copy-start.4
  0.6 4.6 %copy-start.2 = (bf16[1024,144]{0,1:T(8,128)(2,1)S(1)}, bf16[1024,144]{0,1:T(8,128)(2,1)}, u32[]{:S(2)}) copy-start(bf16[1024,144]{0,1:T(8,128)(2,1)} %param.5) | copy-start | bytes 884740
  2.1 0.8 copy-start.3
  5.4 0.7 copy-start
  183.0 1.7 copy-start.1

commit v2 on v1

--- a/solution.py
+++ b/solution.py
@@ -69,7 +69,8 @@
     pl.semaphore_signal(barrier, inc=1, device_id=down, device_id_type=MESH)
     pl.semaphore_wait(barrier, GROUP - 1 + 2)
 
-    images[t] = img_ref[...]
+    for place, owner in enumerate(ORDER):
+        images[t, :, pl.ds(place * SHARE, SHARE)] = img_ref[:, pl.ds(owner * SHARE, SHARE)]
 
     def image_view(way, s, r):
         return images.at[t - s if way == 0 else t + s, :, pl.ds(r * LANES, LANES)]
@@ -77,7 +78,7 @@
     def image_copy(way, s, r):
         view = image_view(way, s, r)
         to = t + 1 if way == 0 else t - 1
-        return copy(view, view, ag_send.at[way, s, r], ag_recv.at[way, s + 1, r], (d, to))
+        return copy(view, view, ag_send.at[way, s], ag_recv.at[way, s + 1, r], (d, to))
 
     def gather_step(pair, s, first=False):
         for r in (2 * pair, 2 * pair + 1):
@@ -121,8 +122,13 @@
         def _():
             text_copy(k).start()
 
-    def hop_out(h):
-        return copy(chain_out.at[h], chain_out.at[h + 1], out_send.at[h], out_recv.at[h + 1], up)
+    def hop_out(h, b):
+        return copy(chain_out.at[h, b], chain_out.at[h + 1, b], out_send.at[h], out_recv.at[h + 1, b], up)
+
+    def pass_out(h):
+        for b in range(STEPS - 1):
+            arrived(chain_out.at[h, b], out_recv.at[h, b])
+            hop_out(h, b).start()
 
     @pl.when(q < GROUP - 3)
     def _():
@@ -132,59 +138,70 @@
     def _():
         arrived(chain_out.at[0, pl.ds(0, 2)], spread_recv)
 
-    hop_out(0).start()
-
-    def first_pair(s, carry):
-        gather_step(0, s)
-        arrived(chain_out.at[s], out_recv.at[s])
-        hop_out(s).start()
-        return carry
-
-    lax.fori_loop(1, N_T, first_pair, 0)
-    gather_step(1, 0, True)
-    arrived(chain_out.at[N_T], out_recv.at[N_T])
-
-    def fan(b, e):
-        k = 1 + b + e
-        return copy(
-            chain_out.at[N_T, b], texts.at[k, strip(q)],
-            fan_send.at[b, e], tx_recv.at[k], (base + e, t),
-        )
-
-    for b, e in PAIRS:
-        @pl.when(q != e)
-        def _():
-            fan(b, e).start()
-
-        @pl.when(q == e)
-        def _():
-            texts[1 + b + e, strip(q), :] = chain_out[N_T, b]
-
-    temper_row = jnp.exp(jnp.full((1, 128), scale_ref[0], jnp.float32))
-    temper = temper_row[:, :1]
-    bias = bias_ref[0]
+    for b in range(STEPS - 1):
+        hop_out(0, b).start()
 
     def text_units(k):
         raw = (txt_ref[...] if k == 0 else texts[k]).astype(jnp.float32)
         scales = lax.rsqrt(jnp.sum(raw * raw, axis=1, keepdims=True) + epsilon)
         return raw * scales, scales
 
-    for k in range(STEPS):
-        if k > 0:
-            @pl.when(q >= k)
-            def _():
-                arrived(texts.at[k], tx_recv.at[k])
-
-            @pl.when(q < k)
-            def _():
-                arrived(texts.at[k, pl.ds(0, SHARE - STRIP)], tx_recv.at[k])
-
+    def text_low(k):
         units, _ = text_units(k)
         low[pl.ds(k * SHARE, SHARE), :] = units.astype(jnp.bfloat16)
         low_t[:, pl.ds(k * SHARE, SHARE)] = units.T.astype(jnp.bfloat16)
+
+    text_low(0)
     delta[...] = jnp.zeros_like(delta)
     cross[...] = jnp.zeros_like(cross)
     loss[...] = jnp.zeros_like(loss)
+
+    def first_pair(s, carry):
+        pass_out(s)
+        gather_step(0, s)
+        return carry
+
+    lax.fori_loop(1, N_T, first_pair, 0)
+    gather_step(1, 0, True)
+
+    def fan(b, e):
+        k = 1 + b + e
+        return copy(
+            chain_out.at[N_T, b], texts.at[k, strip(q)],
+            fan_send.at[b, e], tx_recv.at[k], (base + e, t),
+        )
+
+    for b, e in PAIRS:
+        if e == 0:
+            arrived(chain_out.at[N_T, b], out_recv.at[N_T, b])
+
+        @pl.when(q != e)
+        def _():
+            fan(b, e).start()
+
+        @pl.when(q == e)
+        def _():
+            texts[1 + b + e, strip(q), :] = chain_out[N_T, b]
+
+    gather_step(1, 1)
+
+    temper_row = jnp.exp(jnp.full((1, 128), scale_ref[0], jnp.float32))
+    temper = temper_row[:, :1]
+    bias = bias_ref[0]
+
+    for k in range(1, STEPS):
+        @pl.when(q >= k)
+        def _():
+            arrived(texts.at[k], tx_recv.at[k])
+
+        @pl.when(q < k)
+        def _():
+            arrived(texts.at[k, pl.ds(0, SHARE - STRIP)], tx_recv.at[k])
+
+        text_low(k)
+
+    def lane_block(owner):
+        return pl.ds(pl.multiple_of(owner * SHARE, SHARE), SHARE)
 
     def compute(r, carry):
         lanes = pl.ds(pl.multiple_of(r * LANES, LANES), LANES)
@@ -197,7 +214,8 @@
         block = d - step
         block = jnp.where(block < 0, block + N_DP, block)
         names = block * ROWS + t * SHARE + (index - step * SHARE)
-        same = partner_ref[:, lanes] == names
+        pairs = jnp.concatenate([partner_ref[:, lane_block(N_T - 1 - r)], partner_ref[:, lane_block(r)]], axis=1)
+        same = pairs == names
         logits = temper * dots + bias
         z = jnp.where(same, -logits, logits)
         e = jnp.exp(z)
@@ -227,7 +245,7 @@
         to = t + 1 if way == 0 else t - 1
         return copy(
             piece.at[owner, sum_rows(m)], held.at[owner, sum_rows(m)],
-            rs_send.at[way, owner, m], rs_recv.at[way, owner, m], (d, to),
+            rs_send.at[way, owner], rs_recv.at[way, owner, m], (d, to),
         )
 
     def sum_take(way, owner, m):
@@ -260,19 +278,22 @@
         return carry
 
     def second_pair(c, carry):
-        gather_step(1, 2 * c + 1)
         compute(c, 0)
         gather_step(1, 2 * c + 2)
-        return lax.fori_loop(4 * c, 4 * c + 4, reduce_step, carry)
+        lax.fori_loop(4 * c, 4 * c + 4, reduce_step, 0)
+        gather_step(1, 2 * c + 3)
+        return carry
 
     lax.fori_loop(0, 2, second_pair, 0)
 
     def last_slices(s, carry):
         gather_step(1, s)
-        return lax.fori_loop(2 * s - 2, 2 * s, reduce_step, carry)
-
-    lax.fori_loop(5, N_T, last_slices, 0)
-    lax.fori_loop(2, 4, compute, 0)
+        return lax.fori_loop(3 * s - 10, 3 * s - 7, reduce_step, carry)
+
+    lax.fori_loop(6, N_T, last_slices, 0)
+    compute(2, 0)
+    lax.fori_loop(14, 18, reduce_step, 0)
+    compute(3, 0)
 
     def text_result(k):
         rows = pl.ds(k * SHARE, SHARE)
@@ -305,14 +326,17 @@
                         share_copy(k, slot, other).start()
                     shares[slot] = contrib[k, strip(q), :]
 
-        @pl.when(q >= k)
-        def _():
-            grad_copy(k).start()
-
-    lax.fori_loop(14, 20, reduce_step, 0)
-
-    def hop_back(h):
-        return copy(chain_back.at[h], chain_back.at[h + 1], back_send.at[h], back_recv.at[h + 1], down)
+    lax.fori_loop(18, 22, reduce_step, 0)
+
+    def hop_back(h, b):
+        return copy(
+            chain_back.at[h, b], chain_back.at[h + 1, b], back_send.at[h], back_recv.at[h + 1, b], down
+        )
+
+    def pass_back(h):
+        for b in range(STEPS - 1):
+            arrived(chain_back.at[h, b], back_recv.at[h, b])
+            hop_back(h, b).start()
 
     for e in range(STEPS - 1):
         @pl.when(q == e)
@@ -330,40 +354,46 @@
                 term = shares[slot].astype(jnp.float32)
                 total = term if total is None else total + term
         chain_back[0, b] = total.astype(jnp.bfloat16)
-    hop_back(0).start()
-
-    def tail(h, carry):
-        lax.fori_loop(17 + 3 * h, 20 + 3 * h, reduce_step, carry)
-        arrived(chain_back.at[h], back_recv.at[h])
-        hop_back(h).start()
-        return carry
-
-    lax.fori_loop(1, N_T, tail, 0)
-    lax.fori_loop(41, WINDOW_STEPS, reduce_step, 0)
-    arrived(chain_back.at[N_T], back_recv.at[N_T])
-
-    def home(b):
-        return copy(
-            chain_back.at[N_T, b], returned.at[3, strip(q)],
-            home_send.at[b], gr_recv.at[3], (base + GROUP - 1 - b, t),
-        )
-
-    for b in range(STEPS - 1):
-        @pl.when(q != GROUP - 1 - b)
-        def _():
-            home(b).start()
-
-        @pl.when(q == GROUP - 1 - b)
-        def _():
-            returned[3, strip(q), :] = chain_back[N_T, b]
-
-    image_out[...] = piece[t].astype(jnp.float32).T.astype(jnp.bfloat16)
+        hop_back(0, b).start()
+
+    for k in range(1, STEPS):
+        @pl.when(q >= k)
+        def _():
+            grad_copy(k).start()
 
     grads, total = text_result(0)
     total = jnp.broadcast_to(total, (SHARE, 128))
     delta[pl.ds(0, SHARE), :] = grads
     loss[pl.ds(0, SHARE), :] = total
 
+    def tail(h, carry):
+        lax.fori_loop(20 + 2 * h, 22 + 2 * h, reduce_step, carry)
+        pass_back(h)
+        return carry
+
+    lax.fori_loop(1, N_T, tail, 0)
+    lax.fori_loop(36, 40, reduce_step, 0)
+
+    def home(b):
+        return copy(
+            chain_back.at[N_T, b], returned.at[3, strip(q)],
+            home_send.at[b], gr_recv.at[3], (base + GROUP - 1 - b, t),
+        )
+
+    for b in range(STEPS - 1):
+        arrived(chain_back.at[N_T, b], back_recv.at[N_T, b])
+
+        @pl.when(q != GROUP - 1 - b)
+        def _():
+            home(b).start()
+
+        @pl.when(q == GROUP - 1 - b)
+        def _():
+            returned[3, strip(q), :] = chain_back[N_T, b]
+
+    lax.fori_loop(40, WINDOW_STEPS, reduce_step, 0)
+    image_out[...] = piece[t].astype(jnp.float32).T.astype(jnp.bfloat16)
+
     def take(k):
         delta[pl.ds(0, SHARE), :] += returned[k, :, pl.ds(0, WIDTH)].astype(jnp.float32)
         loss[pl.ds(0, SHARE), :] += returned[k, :, pl.ds(WIDTH, 128)].astype(jnp.float32)
@@ -384,7 +414,7 @@
 
     take(3)
     text_out[...] = delta[pl.ds(0, SHARE), :].astype(jnp.bfloat16)
-    loss_out[...] = loss[pl.ds(0, SHARE), :].T[:8]
+    loss_out[...] = loss[pl.ds(0, SHARE), :].T[:1]
 
     @pl.when(q >= GROUP - 3)
     def _():
@@ -414,25 +444,24 @@
             grad_copy(k).wait_send()
 
     def drain(s, carry):
-        hop_out(s).wait_send()
-        hop_back(s).wait_send()
-        for r in range(CHUNKS):
-            @pl.when(jnp.logical_and(t >= s, t < N_T - 1))
-            def _():
-                image_copy(0, s, r).wait_send()
-
-            @pl.when(jnp.logical_and(t + s < N_T, t > 0))
-            def _():
-                image_copy(1, s, r).wait_send()
-
-        for m in range(PARTS):
-            @pl.when(s > t)
-            def _():
-                sum_copy(0, s, m).wait_send()
-
-            @pl.when(s < t)
-            def _():
-                sum_copy(1, s, m).wait_send()
+        left(chain_out.at[s], out_send.at[s])
+        left(chain_back.at[s], back_send.at[s])
+
+        @pl.when(jnp.logical_and(t >= s, t < N_T - 1))
+        def _():
+            left(images.at[s], ag_send.at[0, s])
+
+        @pl.when(jnp.logical_and(t + s < N_T, t > 0))
+        def _():
+            left(images.at[s], ag_send.at[1, s])
+
+        @pl.when(s > t)
+        def _():
+            left(piece.at[s], rs_send.at[0, s])
+
+        @pl.when(s < t)
+        def _():
+            left(piece.at[s], rs_send.at[1, s])
 
         return carry
 
@@ -440,10 +469,8 @@
 
 
 def local(image_emb, text_emb, partner, log_scale, logit_bias):
-    by_owner = image_emb.reshape(N_T, SHARE, SLICE)
-    ordered = jnp.concatenate([by_owner[o] for o in ORDER], axis=0).T
-    pairs = partner.reshape(N_T, SHARE)
-    pairs = jnp.concatenate([pairs[o] for o in ORDER]).reshape(1, ROWS)
+    ordered = image_emb.T
+    pairs = partner.reshape(1, ROWS)
     bf16, f32 = jnp.bfloat16, jnp.float32
     dma = pltpu.SemaphoreType.DMA
     vmem = pl.BlockSpec(memory_space=pltpu.VMEM)
@@ -454,7 +481,7 @@
         out_shape=(
             jax.ShapeDtypeStruct((SHARE, WIDTH), bf16),
             jax.ShapeDtypeStruct((SHARE, WIDTH), bf16),
-            jax.ShapeDtypeStruct((8, SHARE), f32),
+            jax.ShapeDtypeStruct((1, SHARE), f32),
         ),
         in_specs=[vmem, vmem, vmem, smem, smem],
         out_specs=(vmem, vmem, vmem),
@@ -474,18 +501,18 @@
             pltpu.VMEM((STEPS, SHARE, CARRY), bf16),
             pltpu.VMEM((STEPS, SHARE, CARRY), bf16),
             pltpu.VMEM((len(PAIRS), STRIP, CARRY), bf16),
-            dma((2, N_T + 1, CHUNKS)), dma((2, N_T + 1, CHUNKS)),
-            dma((2, N_T, PARTS)), dma((2, N_T, PARTS)),
+            dma((2, N_T)), dma((2, N_T + 1, CHUNKS)),
+            dma((2, N_T)), dma((2, N_T, PARTS)),
             dma((STEPS,)), dma((STEPS,)), dma, dma,
-            dma((N_T,)), dma((N_T + 1,)), dma((STEPS - 1, STEPS - 1)),
+            dma((N_T,)), dma((N_T + 1, STEPS - 1)), dma((STEPS - 1, STEPS - 1)),
             dma((STEPS,)), dma((STEPS,)), dma((STEPS,)), dma,
-            dma((N_T,)), dma((N_T + 1,)), dma((STEPS - 1,)),
+            dma((N_T,)), dma((N_T + 1, STEPS - 1)), dma((STEPS - 1,)),
         ],
         compiler_params=pltpu.CompilerParams(
             collective_id=0, has_side_effects=True, vmem_limit_bytes=56 * 2**20
         ),
     )(ordered, text_emb, pairs, log_scale, logit_bias)
-    return image_grad, text_grad, text_loss[0]
+    return image_grad, text_grad, text_loss.reshape(SHARE)
 
 
 def solution(mesh):

time: 186 us -> 165 us (0.89)
  the two profiles are of different devices: /device:TPU:88 before, /device:TPU:152 now
where the time goes in v2:
time: 165 us
  Pallas kernels  160 us (97%)
  local copies, waits for them, and re-layouts  2.98 us (2%)
  between operations  1.94 us (1%)
    pallas_call x1, Pallas kernels, local(): pl.pallas_call(kernel, name='window_loss', out_shape=(jax.ShapeDtypeStruc...  160 us

profile of v2, /device:TPU:152, one launch (start us, length us, event | category | flops | bytes accessed | tf_op | source)
XLA Modules:
  0.0 164.6 jit_solution(15853672338937860976)
XLA Ops:
  1.9 159.6 %window_loss.1 = (bf16[128,1152]{1,0:T(8,128)(2,1)}, bf16[128,1152]{1,0:T(8,128)(2,1)}, f32[1,128]{1,0:T(1,128)}) custom-call(bf16[144,1024]{1,0:T(8,128)(2,1)} %bitcast.3, bf16[128,1152]{1,0:T(8,128)(2,1)} %txt_ref.1, s32[1,1024]{1,0:T(1,128)} %bitcast.4, f32[1]{0:T(128)S(6)} %copy.11.scale_ref, f32[1]{0:T(128)S(6)} %copy.12.bias_ref), custom_call_target="tpu_custom_call" | custom-call | tf_op jit(solution)/shard_map/window_loss/pallas_call | solution.py:478
  161.6 0.0 copy-start
  161.6 1.7 %copy.13 = bf16[128,1152]{1,0:T(8,128)(2,1)} copy(bf16[128,1152]{1,0:T(8,128)(2,1)} %get-tuple-element.12) | data formatting | bytes 589824
  163.3 0.0 copy-done
  163.3 0.0 copy-start.1
  163.3 0.7 copy.14
  164.0 0.0 copy-done.1
  164.0 0.5 copy.15
Async XLA Ops:
  161.6 1.8 %copy-start = (bf16[128,1152]{1,0:T(8,128)(2,1)S(1)}, bf16[128,1152]{1,0:T(8,128)(2,1)}, u32[]{:S(2)}) copy-start(bf16[128,1152]{1,0:T(8,128)(2,1)} %get-tuple-element.13) | copy-start | bytes 884740
  163.3 0.7 copy-start.1

commit v3 on v2

--- a/solution.py
+++ b/solution.py
@@ -367,9 +367,8 @@
     loss[pl.ds(0, SHARE), :] = total
 
     def tail(h, carry):
-        lax.fori_loop(20 + 2 * h, 22 + 2 * h, reduce_step, carry)
         pass_back(h)
-        return carry
+        return lax.fori_loop(20 + 2 * h, 22 + 2 * h, reduce_step, carry)
 
     lax.fori_loop(1, N_T, tail, 0)
     lax.fori_loop(36, 40, reduce_step, 0)

time: 165 us -> 166 us (level)
  no operation moved by 1% of the time
where the time goes in v3:
time: 166 us
  Pallas kernels  161 us (97%)
  local copies, waits for them, and re-layouts  2.98 us (2%)
  between operations  1.94 us (1%)
    pallas_call x1, Pallas kernels, local(): pl.pallas_call(kernel, name='window_loss', out_shape=(jax.ShapeDtypeStruc...  161 us

profile of v3, /device:TPU:152, one launch (start us, length us, event | category | flops | bytes accessed | tf_op | source)
XLA Modules:
  0.0 165.5 jit_solution(14578398133841175303)
XLA Ops:
  1.9 160.6 %window_loss.1 = (bf16[128,1152]{1,0:T(8,128)(2,1)}, bf16[128,1152]{1,0:T(8,128)(2,1)}, f32[1,128]{1,0:T(1,128)}) custom-call(bf16[144,1024]{1,0:T(8,128)(2,1)} %bitcast.3, bf16[128,1152]{1,0:T(8,128)(2,1)} %txt_ref.1, s32[1,1024]{1,0:T(1,128)} %bitcast.4, f32[1]{0:T(128)S(6)} %copy.11.scale_ref, f32[1]{0:T(128)S(6)} %copy.12.bias_ref), custom_call_target="tpu_custom_call" | custom-call | tf_op jit(solution)/shard_map/window_loss/pallas_call | solution.py:477
  162.6 0.0 copy-start
  162.6 1.7 %copy.13 = bf16[128,1152]{1,0:T(8,128)(2,1)} copy(bf16[128,1152]{1,0:T(8,128)(2,1)} %get-tuple-element.12) | data formatting | bytes 589824
  164.3 0.0 copy-done
  164.3 0.0 copy-start.1
  164.3 0.7 copy.14
  165.0 0.0 copy-done.1
  165.0 0.5 copy.15
Async XLA Ops:
  162.6 1.8 %copy-start = (bf16[128,1152]{1,0:T(8,128)(2,1)S(1)}, bf16[128,1152]{1,0:T(8,128)(2,1)}, u32[]{:S(2)}) copy-start(bf16[128,1152]{1,0:T(8,128)(2,1)} %get-tuple-element.13) | copy-start | bytes 884740
  164.3 0.7 copy-start.1
